TPU v7x, 256 devices: a whole 4x4x8 slice. The times are simulated.
256 devices in a mesh: row: 16 (over x, z_lo), col: 16 (over z_hi, y, core).
Axes of the slice: x: 4, y: 4, z: 8 (z_hi: 2, z_lo: 4; z = z_hi * 4 + z_lo), core: 2. Of those that a mesh axis runs over, the one named last changes fastest.
Arguments:
- panel: float32 [4, 49152, 256], P(None, 'row', 'col'), may hold values from -0.02734375 to 0.02734375
- t_factor: float32 [4, 256, 256], replicated, may hold values from -6 to 6
- eigvecs: float32 [49152, 4096], P('row', 'col'), may hold values from -2000 to 2000, as said below
Outputs:
- regrouped: float32 [49152, 4096], P('row', 'col')
Inputs may be any that keep to these rules, and one draw needn't show every extreme that they name: `eigvecs`: Real-valued entries.
All inputs are finite; a program needn't handle non-finite values.
Results may differ from a plain program's by a relative error of at most 0.00014.
Values sent between devices are 32-bit elements; how exact they have to be, the bound alone decides.
A program may use at most 64 MiB of HBM per device.

v0:
```python
import functools

import jax
import jax.numpy as jnp
from jax import lax
from jax.experimental import pallas as pl
from jax.experimental.pallas import tpu as pltpu
from jax.sharding import PartitionSpec as P

MESH = pl.DeviceIdType.MESH
F32 = jnp.float32
BF16 = jnp.bfloat16
NT = (((1,), (1,)), ((), ()))
NN = (((1,), (0,)), ((), ()))
CHUNK = 1024


def split(x):
    high = x.astype(BF16)
    return high, (x - high.astype(F32)).astype(BF16)


def dot3(ah, al, bh, bl, dims):
    dot = functools.partial(lax.dot_general, dimension_numbers=dims, preferred_element_type=F32)
    return dot(ah, bh) + dot(ah, bl) + dot(al, bh)


def kernel(
    total_rows, v_hbm, t_hbm, z_hbm, o_ref,
    zin, tin, vg, vh, vl, u, uh, ul, acc, gram, pt, rx, rz, ct, out, nsrc, nrecv, scl, sclr,
    loc, z_s, z_r, y_s, y_r, k_s, k_r, r_s, r_r, a_s, a_r, n_s, n_r, s_s, s_r, o_s,
):
    panels, nb, lanes = vg.shape
    half = u.shape[0] // 2
    own = half // 4
    row, col = lax.axis_index("row"), lax.axis_index("col")
    xi, zi = row // 4, row % 4
    hi, yi, ki = col // 8, (col // 2) % 4, col % 2

    def chip(h, y, k):
        return (row, h * 8 + y * 2 + k)

    z_peer = chip(1 - hi, yi, ki)
    k_peer = chip(hi, yi, 1 - ki)
    right, left, far = (yi + 1) % 4, (yi + 3) % 4, (yi + 2) % 4
    y_right, y_left = chip(hi, right, ki), chip(hi, left, ki)

    def at(p, h, y, start=0, size=16):
        return vg.at[p, pl.ds(pl.multiple_of((h * 8 + y * 2 + ki) * 16 + start, 8), size)]

    def remote(src, dst, send, recv, device):
        return pltpu.make_async_remote_copy(
            src_ref=src, dst_ref=dst, send_sem=send, recv_sem=recv, device_id=device, device_id_type=MESH
        )

    def own_copy(p):
        return pltpu.make_async_copy(v_hbm.at[p], at(p, hi, yi), loc.at[p])

    def z_copy(p):
        return remote(v_hbm.at[p], at(p, hi, yi), z_s.at[p], z_r.at[p], z_peer)

    def side(s):
        return hi if s == 0 else 1 - hi

    def y_copy(p, s, kind):
        h = side(s)
        if kind == 0:
            block, device = at(p, h, yi), y_right
        elif kind == 1:
            block, device = at(p, h, yi), y_left
        elif kind == 2:
            block, device = at(p, h, left, 0, 8), y_right
        else:
            block, device = at(p, h, right, 8, 8), y_left
        i = s * 4 + kind
        return remote(block, block, y_s.at[p, i], y_r.at[p, i], device)

    def k_copy(p, s, which):
        block = at(p, side(s), (yi, left, right, far)[which])
        i = s * 4 + which
        return remote(block, block, k_s.at[p, i], k_r.at[p, i], k_peer)

    def row_peer(dx, dz):
        return (((xi + dx) % 4) * 4 + (zi + dz) % 4, col)

    def part(ref, p, h, x):
        return ref.at[p, pl.ds(pl.multiple_of(h * half + x * own, 8), own)]

    def rs_x(p, h, i):
        to = (xi + i) % 4
        j = h * 9 + i - 1
        return remote(part(pt, p, h, to), rx.at[p, h, i - 1], r_s.at[p, j], r_r.at[p, j], row_peer(i, 0))

    def ex_z(p, h, i):
        j = h * 9 + 2 + i
        block = rz.at[p, h, zi]
        return remote(block, block, r_s.at[p, j], r_r.at[p, j], row_peer(0, i))

    def ag_x(p, h, i):
        j = h * 9 + 5 + i
        block = part(ct, p, h, xi)
        return remote(block, block, r_s.at[p, j], r_r.at[p, j], row_peer(i, 0))

    def regroup(i):
        to = col ^ i
        return remote(
            u.at[pl.ds(pl.multiple_of(to * 16, 16), 16)],
            out.at[pl.ds(pl.multiple_of(col * 16, 16), 16)],
            a_s.at[i], a_r.at[i], (row, to),
        )

    def norms(i):
        return remote(nsrc, nrecv.at[i], n_s.at[i], n_r.at[i], ((row + i) % 16, col))

    def scales(i):
        to = col ^ i
        return remote(
            scl.at[pl.ds(pl.multiple_of(to * 16, 16), 16)],
            sclr.at[pl.ds(pl.multiple_of(col * 16, 16), 16)],
            s_s.at[i], s_r.at[i], (row, to),
        )

    z_load = pltpu.make_async_copy(z_hbm, zin, loc.at[panels])
    t_load = pltpu.make_async_copy(t_hbm, tin, loc.at[panels + 1])
    for p in range(panels):
        own_copy(p).start()
    z_load.start()
    t_load.start()
    barrier = pltpu.get_barrier_semaphore()

    def greet(i, carry):
        pl.semaphore_signal(barrier, inc=1, device_id=((row + i) % 16, col), device_id_type=MESH)
        pl.semaphore_signal(barrier, inc=1, device_id=(row, (col + i) % 16), device_id_type=MESH)
        return carry

    lax.fori_loop(1, 16, greet, 0)
    for p in range(panels):
        own_copy(p).wait()
    pl.semaphore_wait(barrier, 30)

    def stage_own(p):
        y_copy(p, 0, 0).start()
        y_copy(p, 0, 1).start()
        k_copy(p, 0, 0).start()

    def stage_peer(p):
        z_copy(p).wait_recv()
        y_copy(p, 1, 0).start()
        y_copy(p, 1, 1).start()
        k_copy(p, 1, 0).start()

    def stage_relay(p, s):
        y_copy(p, s, 0).wait_recv()
        y_copy(p, s, 2).start()
        k_copy(p, s, 1).start()
        y_copy(p, s, 1).wait_recv()
        y_copy(p, s, 3).start()
        k_copy(p, s, 2).start()

    def stage_far(p, s):
        y_copy(p, s, 2).wait_recv()
        y_copy(p, s, 3).wait_recv()
        k_copy(p, s, 3).start()

    def stage_end(p):
        for s in range(2):
            for which in range(4):
                k_copy(p, s, which).wait_recv()

    def chunks(body):
        @pl.loop(0, lanes // CHUNK)
        def _(i):
            body(pl.ds(pl.multiple_of(i * CHUNK, CHUNK), CHUNK))

    z_copy(0).start()
    stage_own(0)
    stage_own(1)

    z_load.wait()
    t_load.wait()

    @pl.loop(0, lanes // 512)
    def _(i):
        s = pl.ds(pl.multiple_of(i * 512, 512), 512)
        block = zin[s, :].T
        u[:, s] = block
        high, low = split(block)
        uh[:, s] = high
        ul[:, s] = low

    stage_relay(0, 0)
    stage_peer(0)
    z_copy(1).start()
    z_copy(2).start()
    stage_relay(1, 0)
    stage_far(0, 0)
    stage_relay(0, 1)
    stage_own(2)
    stage_peer(1)
    z_copy(3).start()
    stage_far(0, 1)
    stage_end(0)

    upper = lax.broadcasted_iota(jnp.int32, (nb, nb), 0) <= lax.broadcasted_iota(jnp.int32, (nb, nb), 1)

    def apply(p, keep):
        ch, cl = split(ct[p])

        def body(s):
            new = u[:, s] - dot3(ch, cl, vh[p, :, s], vl[p, :, s], NN)
            u[:, s] = new
            if keep:
                high, low = split(new)
                uh[:, s] = high
                ul[:, s] = low

        chunks(body)

    @pl.loop(0, panels)
    def _(p):
        @pl.loop(0, nb // 16)
        def _(i):
            s = pl.ds(pl.multiple_of(i * 16, 16), 16)
            high, low = split(vg[p, s, :])
            vh[p, s, :] = high
            vl[p, s, :] = low

        acc[...] = dot3(uh[...], ul[...], vh[p], vl[p], NT)

        @pl.when(p > 0)
        def _():
            gram[...] = dot3(vh[p - 1], vl[p - 1], vh[p], vl[p], NT)
            for h in range(2):
                for i in range(1, 4):
                    ag_x(p - 1, h, i).wait_recv()
            ch, cl = split(ct[p - 1])
            gh, gl = split(gram[...])
            acc[...] -= dot3(ch, cl, gh, gl, NN)

        pt[p] = acc[...]
        for h in range(2):
            for i in range(1, 4):
                rs_x(p, h, i).start()

        @pl.when(p < panels - 1)
        def _():
            stage_relay(p + 1, 1)

        @pl.when(p < panels - 2)
        def _():
            stage_relay(p + 2, 0)

        @pl.when(p > 0)
        def _():
            apply(p - 1, True)

        for h in range(2):
            for i in range(1, 4):
                rs_x(p, h, i).wait_recv()
            mine = pl.ds(pl.multiple_of(h * half + xi * own, 8), own)
            rz[p, h, zi] = pt[p, mine] + (rx[p, h, 0] + rx[p, h, 1] + rx[p, h, 2])
            for i in range(1, 4):
                ex_z(p, h, i).start()

        @pl.when(p < panels - 2)
        def _():
            stage_peer(p + 2)

        th, tl = split(jnp.where(upper, tin[p], 0.0))
        for h in range(2):
            for i in range(1, 4):
                ex_z(p, h, i).wait_recv()
            mh, ml = split((rz[p, h, 0] + rz[p, h, 1]) + (rz[p, h, 2] + rz[p, h, 3]))
            mine = pl.ds(pl.multiple_of(h * half + xi * own, 8), own)
            ct[p, mine] = dot3(mh, ml, th, tl, NT)
            for i in range(1, 4):
                ag_x(p, h, i).start()

        @pl.when(p < panels - 3)
        def _():
            stage_own(p + 3)

        @pl.when(p < panels - 1)
        def _():
            stage_far(p + 1, 0)
            stage_far(p + 1, 1)
            stage_end(p + 1)

    for h in range(2):
        for i in range(1, 4):
            ag_x(panels - 1, h, i).wait_recv()
    apply(panels - 1, False)

    def each(first, body):
        def step(i, carry):
            body(i)
            return carry

        lax.fori_loop(first, 16, step, 0)

    squares = jnp.zeros((nb, 128), F32)
    for i in range(lanes // 128):
        block = u[:, i * 128 : (i + 1) * 128]
        squares += block * block
    partial = jnp.broadcast_to(jnp.sum(squares.T, axis=0, keepdims=True), (8, nb))
    nsrc[...] = partial
    nrecv[0] = partial
    each(1, lambda i: norms(i).start())
    each(1, lambda i: regroup(16 - i).start())
    each(1, lambda i: norms(i).wait_recv())
    norm_sq = jnp.sum(nrecv[...], axis=0)
    tall = jnp.broadcast_to(norm_sq[0:1], (128, nb)).T
    scl[...] = lax.rsqrt(tall / total_rows + 1e-06)
    each(1, lambda i: scales(i).start())

    def there(source):
        return pl.ds(pl.multiple_of(source * 16, 16), 16)

    def store(source):
        return pltpu.make_async_copy(out.at[there(source)], o_ref.at[there(source)], o_s.at[source])

    out[there(col), :] = u[there(col), :] * scl[there(col), 0:1]
    store(col).start()

    def take(i):
        source = col ^ i
        scales(i).wait_recv()
        regroup(i).wait_recv()
        out[there(source), :] = out[there(source), :] * sclr[there(source), 0:1]
        store(source).start()

    each(1, take)
    store(col).wait()
    each(1, lambda i: store(col ^ i).wait())

    def sent(i):
        regroup(i).wait_send()
        norms(i).wait_send()
        scales(i).wait_send()

    each(1, sent)

    @pl.loop(0, panels)
    def _(p):
        z_copy(p).wait_send()
        for s in range(2):
            for kind in range(4):
                y_copy(p, s, kind).wait_send()
                k_copy(p, s, kind).wait_send()
        for h in range(2):
            for i in range(1, 4):
                rs_x(p, h, i).wait_send()
                ex_z(p, h, i).wait_send()
                ag_x(p, h, i).wait_send()


def local(panel, t_factor, eigvecs):
    panels, lanes, width = panel.shape
    cols = eigvecs.shape[1]
    nb = t_factor.shape[1]
    vt = jnp.transpose(panel, (0, 2, 1))
    total_rows = lanes * lax.axis_size("row")
    vmem, dma = pltpu.VMEM, pltpu.SemaphoreType.DMA
    any_spec = pl.BlockSpec(memory_space=pl.ANY)
    done = pl.pallas_call(
        functools.partial(kernel, total_rows),
        out_shape=jax.ShapeDtypeStruct((cols, lanes), F32),
        in_specs=[any_spec] * 3,
        out_specs=any_spec,
        scratch_shapes=[
            vmem((lanes, cols), F32),
            vmem((panels, nb, nb), F32),
            vmem((panels, nb, lanes), F32),
            vmem((panels, nb, lanes), BF16),
            vmem((panels, nb, lanes), BF16),
            vmem((cols, lanes), F32),
            vmem((cols, lanes), BF16),
            vmem((cols, lanes), BF16),
            vmem((cols, nb), F32),
            vmem((nb, nb), F32),
            vmem((panels, cols, nb), F32),
            vmem((panels, 2, 3, cols // 8, nb), F32),
            vmem((panels, 2, 4, cols // 8, nb), F32),
            vmem((panels, cols, nb), F32),
            vmem((cols, lanes), F32),
            vmem((8, cols), F32),
            vmem((16, 8, cols), F32),
            vmem((cols, 128), F32),
            vmem((cols, 128), F32),
            dma((panels + 2,)),
            dma((panels,)),
            dma((panels,)),
            dma((panels, 8)),
            dma((panels, 8)),
            dma((panels, 8)),
            dma((panels, 8)),
            dma((panels, 18)),
            dma((panels, 18)),
            dma((16,)),
            dma((16,)),
            dma((16,)),
            dma((16,)),
            dma((16,)),
            dma((16,)),
            dma((16,)),
        ],
        compiler_params=pltpu.CompilerParams(
            collective_id=0, has_side_effects=True, vmem_limit_bytes=60 * 2**20
        ),
    )(vt, t_factor, eigvecs)
    return jnp.transpose(done)


def solution(mesh):
    in_specs = (P(None, "row", "col"), P(), P("row", "col"))
    return jax.shard_map(local, mesh=mesh, in_specs=in_specs, out_specs=P("row", "col"), check_vma=False)
```

profile of v0, /device:TPU:1, one launch (start us, length us, event | category | flops | bytes accessed | tf_op | source)
XLA Modules:
  0.0 197.7 jit_solution(4393288824821072944)
XLA Ops:
  0.0 194.2 %shard_map.37 = f32[256,3072]{1,0:T(8,128)} custom-call(f32[4,16,3072]{2,1,0:T(8,128)} %bitcast.3, f32[4,256,256]{2,1,0:T(8,128)} %t_hbm.1, f32[3072,256]{1,0:T(8,128)} %z_hbm.1), custom_call_target="tpu_custom_call" | custom-call | tf_op jit(solution)/shard_map/pallas_call | solution.py:365
  194.2 3.5 %copy.4 = f32[3072,256]{1,0:T(8,128)} copy(f32[3072,256]{0,1:T(8,128)} %bitcast.2) | data formatting | bytes 6291456 | tf_op jit(solution)/shard_map/transpose | solution.py:411
where the time goes:
time: 201 us; the launch traced here: 198 us
  Pallas kernels  194 us (97%)
  local copies, waits for them, and re-layouts  3.55 us (2%)
    pallas_call x1, Pallas kernels, local(): pl.pallas_call(functools.partial(kernel, total_rows), out_shape=jax.Shape...  194 us

commit v1 on v0

--- a/solution.py
+++ b/solution.py
@@ -27,8 +27,8 @@
 
 def kernel(
     total_rows, v_hbm, t_hbm, z_hbm, o_ref,
-    zin, tin, vg, vh, vl, u, uh, ul, acc, gram, pt, rx, rz, ct, out, nsrc, nrecv, scl, sclr,
-    loc, z_s, z_r, y_s, y_r, k_s, k_r, r_s, r_r, a_s, a_r, n_s, n_r, s_s, s_r, o_s,
+    zin, tin, vg, vh, vl, u, uh, ul, acc, gram, pt, rx, rz, ct, early, ua, ca, out, nsrc, nrecv, scl, sclr,
+    loc, z_s, z_r, y_s, y_r, k_s, k_r, r_s, r_r, a_s, a_r, n_s, n_r, s_s, s_r, o_s, e_s, e_r, c_s, c_r,
 ):
     panels, nb, lanes = vg.shape
     half = u.shape[0] // 2
@@ -36,6 +36,7 @@
     row, col = lax.axis_index("row"), lax.axis_index("col")
     xi, zi = row // 4, row % 4
     hi, yi, ki = col // 8, (col // 2) % 4, col % 2
+    ci = col % 8
 
     def chip(h, y, k):
         return (row, h * 8 + y * 2 + k)
@@ -101,13 +102,27 @@
         block = part(ct, p, h, xi)
         return remote(block, block, r_s.at[p, j], r_r.at[p, j], row_peer(i, 0))
 
-    def regroup(i):
+    def eight(i):
+        return pl.ds(pl.multiple_of(i * 8, 8), 8)
+
+    def sixteen(i):
+        return pl.ds(pl.multiple_of(i * 16, 16), 16)
+
+    def across(i):
+        return (1 - hi) * 8 + (ci ^ i)
+
+    def move_soon(i):
+        return remote(early.at[eight(ci ^ i)], ua.at[eight(ci)], e_s.at[i], e_r.at[i], (row, across(i)))
+
+    def coef(p, i):
+        return remote(ct.at[p, eight(across(i) * 2)], ca.at[p, eight(ci)], c_s.at[p, i], c_r.at[p, i], (row, across(i)))
+
+    def move_across(i):
+        return remote(u.at[eight(across(i) * 2 + 1)], out.at[eight(col * 2 + 1)], a_s.at[8 + i], a_r.at[8 + i], (row, across(i)))
+
+    def move_beside(i):
         to = col ^ i
-        return remote(
-            u.at[pl.ds(pl.multiple_of(to * 16, 16), 16)],
-            out.at[pl.ds(pl.multiple_of(col * 16, 16), 16)],
-            a_s.at[i], a_r.at[i], (row, to),
-        )
+        return remote(u.at[sixteen(to)], out.at[sixteen(col)], a_s.at[i], a_r.at[i], (row, to))
 
     def norms(i):
         return remote(nsrc, nrecv.at[i], n_s.at[i], n_r.at[i], ((row + i) % 16, col))
@@ -187,6 +202,8 @@
         high, low = split(block)
         uh[:, s] = high
         ul[:, s] = low
+        crossing = zin[s, pl.ds(pl.multiple_of((1 - hi) * 128, 128), 128)].T.reshape(8, 16, 512)
+        early[:, s] = crossing[:, 0:8].reshape(64, 512)
 
     stage_relay(0, 0)
     stage_peer(0)
@@ -201,6 +218,13 @@
     stage_far(0, 1)
     stage_end(0)
 
+    def each(first, last, body):
+        def step(i, carry):
+            body(i)
+            return carry
+
+        lax.fori_loop(first, last, step, 0)
+
     upper = lax.broadcasted_iota(jnp.int32, (nb, nb), 0) <= lax.broadcasted_iota(jnp.int32, (nb, nb), 1)
 
     def apply(p, keep):
@@ -233,6 +257,7 @@
             for h in range(2):
                 for i in range(1, 4):
                     ag_x(p - 1, h, i).wait_recv()
+            each(0, 8, lambda i: coef(p - 1, i).start())
             ch, cl = split(ct[p - 1])
             gh, gl = split(gram[...])
             acc[...] -= dot3(ch, cl, gh, gl, NN)
@@ -276,6 +301,8 @@
             for i in range(1, 4):
                 ag_x(p, h, i).start()
 
+        each(p * 2, p * 2 + 2, lambda i: move_soon(i).start())
+
         @pl.when(p < panels - 3)
         def _():
             stage_own(p + 3)
@@ -289,14 +316,8 @@
     for h in range(2):
         for i in range(1, 4):
             ag_x(panels - 1, h, i).wait_recv()
+    each(0, 8, lambda i: coef(panels - 1, i).start())
     apply(panels - 1, False)
-
-    def each(first, body):
-        def step(i, carry):
-            body(i)
-            return carry
-
-        lax.fori_loop(first, 16, step, 0)
 
     squares = jnp.zeros((nb, 128), F32)
     for i in range(lanes // 128):
@@ -305,44 +326,71 @@
     partial = jnp.broadcast_to(jnp.sum(squares.T, axis=0, keepdims=True), (8, nb))
     nsrc[...] = partial
     nrecv[0] = partial
-    each(1, lambda i: norms(i).start())
-    each(1, lambda i: regroup(16 - i).start())
-    each(1, lambda i: norms(i).wait_recv())
+    each(1, 16, lambda i: norms(i).start())
+    each(1, 8, lambda i: move_beside(i).start())
+    each(1, 16, lambda i: norms(i).wait_recv())
     norm_sq = jnp.sum(nrecv[...], axis=0)
     tall = jnp.broadcast_to(norm_sq[0:1], (128, nb)).T
     scl[...] = lax.rsqrt(tall / total_rows + 1e-06)
-    each(1, lambda i: scales(i).start())
-
-    def there(source):
-        return pl.ds(pl.multiple_of(source * 16, 16), 16)
+    each(1, 16, lambda i: scales(i).start())
+    each(0, 8, lambda i: move_across(i).start())
+
+    each(0, 8, lambda i: move_soon(i).wait_recv())
+
+    @pl.loop(0, panels)
+    def _(p):
+        each(0, 8, lambda i: coef(p, i).wait_recv())
+        ch, cl = split(ca[p])
+
+        def body(s):
+            ua[:, s] -= dot3(ch, cl, vh[p, :, s], vl[p, :, s], NN)
+
+        chunks(body)
 
     def store(source):
-        return pltpu.make_async_copy(out.at[there(source)], o_ref.at[there(source)], o_s.at[source])
-
-    out[there(col), :] = u[there(col), :] * scl[there(col), 0:1]
+        return pltpu.make_async_copy(out.at[sixteen(source)], o_ref.at[sixteen(source)], o_s.at[source])
+
+    out[sixteen(col), :] = u[sixteen(col), :] * scl[sixteen(col), 0:1]
     store(col).start()
 
-    def take(i):
+    def take_beside(i):
         source = col ^ i
         scales(i).wait_recv()
-        regroup(i).wait_recv()
-        out[there(source), :] = out[there(source), :] * sclr[there(source), 0:1]
+        move_beside(i).wait_recv()
+        out[sixteen(source), :] = out[sixteen(source), :] * sclr[sixteen(source), 0:1]
         store(source).start()
 
-    each(1, take)
-    store(col).wait()
-    each(1, lambda i: store(col ^ i).wait())
+    each(1, 8, take_beside)
+
+    def take_across(i):
+        source = across(i)
+        scales(8 + i).wait_recv()
+        low, high = eight(source * 2), eight(source * 2 + 1)
+        out[low, :] = ua[eight(ci ^ i), :] * sclr[low, 0:1]
+        move_across(i).wait_recv()
+        out[high, :] = out[high, :] * sclr[high, 0:1]
+        store(source).start()
+
+    each(0, 8, take_across)
+    each(0, 16, lambda i: store(i).wait())
 
     def sent(i):
-        regroup(i).wait_send()
         norms(i).wait_send()
         scales(i).wait_send()
 
-    each(1, sent)
+    each(1, 16, sent)
+    each(1, 8, lambda i: move_beside(i).wait_send())
+
+    def sent_across(i):
+        move_soon(i).wait_send()
+        move_across(i).wait_send()
+
+    each(0, 8, sent_across)
 
     @pl.loop(0, panels)
     def _(p):
         z_copy(p).wait_send()
+        each(0, 8, lambda i: coef(p, i).wait_send())
         for s in range(2):
             for kind in range(4):
                 y_copy(p, s, kind).wait_send()
@@ -382,6 +430,9 @@
             vmem((panels, 2, 3, cols // 8, nb), F32),
             vmem((panels, 2, 4, cols // 8, nb), F32),
             vmem((panels, cols, nb), F32),
+            vmem((cols // 4, lanes), F32),
+            vmem((cols // 4, lanes), F32),
+            vmem((panels, cols // 4, nb), F32),
             vmem((cols, lanes), F32),
             vmem((8, cols), F32),
             vmem((16, 8, cols), F32),
@@ -403,6 +454,10 @@
             dma((16,)),
             dma((16,)),
             dma((16,)),
+            dma((8,)),
+            dma((8,)),
+            dma((panels, 8)),
+            dma((panels, 8)),
         ],
         compiler_params=pltpu.CompilerParams(
             collective_id=0, has_side_effects=True, vmem_limit_bytes=60 * 2**20

time: 201 us -> 185 us (0.920); the launches traced: 198 us -> 185 us
  Pallas kernels: 194 us -> 181 us
    pallas_call x1, Pallas kernels: 194 us -> 181 us  [local(): pl.pallas_call(functools.partial(kernel, total_rows), out_shape=jax.Shape...]
where the time goes in v1:
time: 185 us
  Pallas kernels  181 us (98%)
  local copies, waits for them, and re-layouts  3.55 us (2%)
    pallas_call x1, Pallas kernels, local(): pl.pallas_call(functools.partial(kernel, total_rows), out_shape=jax.Shape...  181 us

profile of v1, /device:TPU:1, one launch (start us, length us, event | category | flops | bytes accessed | tf_op | source)
XLA Modules:
  0.0 185.0 jit_solution(6243392171328443158)
XLA Ops:
  0.0 181.4 %shard_map.37 = f32[256,3072]{1,0:T(8,128)} custom-call(f32[4,16,3072]{2,1,0:T(8,128)} %bitcast.3, f32[4,256,256]{2,1,0:T(8,128)} %t_hbm.1, f32[3072,256]{1,0:T(8,128)} %z_hbm.1), custom_call_target="tpu_custom_call" | custom-call | tf_op jit(solution)/shard_map/pallas_call | solution.py:413
  181.5 3.5 %copy.4 = f32[3072,256]{1,0:T(8,128)} copy(f32[3072,256]{0,1:T(8,128)} %bitcast.2) | data formatting | bytes 6291456 | tf_op jit(solution)/shard_map/transpose | solution.py:466

commit v2 on v1

--- a/solution.py
+++ b/solution.py
@@ -187,7 +187,8 @@
         def _(i):
             body(pl.ds(pl.multiple_of(i * CHUNK, CHUNK), CHUNK))
 
-    z_copy(0).start()
+    for p in range(panels):
+        z_copy(p).start()
     stage_own(0)
     stage_own(1)
 
@@ -207,14 +208,11 @@
 
     stage_relay(0, 0)
     stage_peer(0)
-    z_copy(1).start()
-    z_copy(2).start()
     stage_relay(1, 0)
+    stage_own(2)
     stage_far(0, 0)
     stage_relay(0, 1)
-    stage_own(2)
     stage_peer(1)
-    z_copy(3).start()
     stage_far(0, 1)
     stage_end(0)
 
@@ -271,10 +269,6 @@
         def _():
             stage_relay(p + 1, 1)
 
-        @pl.when(p < panels - 2)
-        def _():
-            stage_relay(p + 2, 0)
-
         @pl.when(p > 0)
         def _():
             apply(p - 1, True)
@@ -289,7 +283,11 @@
 
         @pl.when(p < panels - 2)
         def _():
-            stage_peer(p + 2)
+            stage_relay(p + 2, 0)
+
+        @pl.when(p < panels - 3)
+        def _():
+            stage_own(p + 3)
 
         th, tl = split(jnp.where(upper, tin[p], 0.0))
         for h in range(2):
@@ -303,9 +301,9 @@
 
         each(p * 2, p * 2 + 2, lambda i: move_soon(i).start())
 
-        @pl.when(p < panels - 3)
-        def _():
-            stage_own(p + 3)
+        @pl.when(p < panels - 2)
+        def _():
+            stage_peer(p + 2)
 
         @pl.when(p < panels - 1)
         def _():

time: 185 us -> 183 us (0.989)
  Pallas kernels: 181 us -> 179 us
    pallas_call x1, Pallas kernels: 181 us -> 179 us  [local(): pl.pallas_call(functools.partial(kernel, total_rows), out_shape=jax.Shape...]
where the time goes in v2:
time: 183 us
  Pallas kernels  179 us (98%)
  local copies, waits for them, and re-layouts  3.55 us (2%)
    pallas_call x1, Pallas kernels, local(): pl.pallas_call(functools.partial(kernel, total_rows), out_shape=jax.Shape...  179 us

profile of v2, /device:TPU:1, one launch (start us, length us, event | category | flops | bytes accessed | tf_op | source)
XLA Modules:
  0.0 182.6 jit_solution(16184151161175248562)
XLA Ops:
  0.0 179.1 %shard_map.37 = f32[256,3072]{1,0:T(8,128)} custom-call(f32[4,16,3072]{2,1,0:T(8,128)} %bitcast.3, f32[4,256,256]{2,1,0:T(8,128)} %t_hbm.1, f32[3072,256]{1,0:T(8,128)} %z_hbm.1), custom_call_target="tpu_custom_call" | custom-call | tf_op jit(solution)/shard_map/pallas_call | solution.py:411
  179.1 3.5 %copy.4 = f32[3072,256]{1,0:T(8,128)} copy(f32[3072,256]{0,1:T(8,128)} %bitcast.2) | data formatting | bytes 6291456 | tf_op jit(solution)/shard_map/transpose | solution.py:464

commit v3 on v2

--- a/solution.py
+++ b/solution.py
@@ -255,7 +255,6 @@
             for h in range(2):
                 for i in range(1, 4):
                     ag_x(p - 1, h, i).wait_recv()
-            each(0, 8, lambda i: coef(p - 1, i).start())
             ch, cl = split(ct[p - 1])
             gh, gl = split(gram[...])
             acc[...] -= dot3(ch, cl, gh, gl, NN)
@@ -271,6 +270,7 @@
 
         @pl.when(p > 0)
         def _():
+            each(0, 8, lambda i: coef(p - 1, i).start())
             apply(p - 1, True)
 
         for h in range(2):

time: 183 us -> 181 us (0.989)
  the two profiles are of different devices: /device:TPU:1 before, /device:TPU:9 now
where the time goes in v3:
time: 181 us
  Pallas kernels  178 us (98%)
  local copies, waits for them, and re-layouts  3.55 us (2%)
    pallas_call x1, Pallas kernels, local(): pl.pallas_call(functools.partial(kernel, total_rows), out_shape=jax.Shape...  178 us

profile of v3, /device:TPU:9, one launch (start us, length us, event | category | flops | bytes accessed | tf_op | source)
XLA Modules:
  0.0 181.4 jit_solution(3343777603617445369)
XLA Ops:
  0.0 177.8 %shard_map.37 = f32[256,3072]{1,0:T(8,128)} custom-call(f32[4,16,3072]{2,1,0:T(8,128)} %bitcast.3, f32[4,256,256]{2,1,0:T(8,128)} %t_hbm.1, f32[3072,256]{1,0:T(8,128)} %z_hbm.1), custom_call_target="tpu_custom_call" | custom-call | tf_op jit(solution)/shard_map/pallas_call | solution.py:411
  177.9 3.5 %copy.4 = f32[3072,256]{1,0:T(8,128)} copy(f32[3072,256]{0,1:T(8,128)} %bitcast.2) | data formatting | bytes 6291456 | tf_op jit(solution)/shard_map/transpose | solution.py:464
